TPU v7x, 512 devices: a whole 4x4x16 slice. The times are simulated.
512 devices in a mesh: row: 64 (over y, z), col: 8 (over x, core).
Axes of the slice: x: 4, y: 4, z: 16, core: 2. Of those that a mesh axis runs over, the one named last changes fastest.
Arguments:
- source_points: bfloat16 [8192, 128], P('row'), may hold values from -2.375 to 2.375
- target_points: bfloat16 [131072, 128], P(('col', 'row')), may hold values from -2.375 to 2.375
- source_mass: float32 [64, 128], P('row'), may hold values from 0.5 to 2
- target_mass: float32 [1024, 128], P('col'), may hold values from 0.5 to 2
- tile_list: int32 [64, 8, 2, 16], P('row', 'col'), may hold values from 0 to 127, as said below
- tile_count: int32 [64, 8], P('row', 'col'), may hold values from 1 to 16, as said below
Outputs:
- source_potential: float32 [64, 128], P('row')
- target_potential: float32 [1024, 128], P('col')
Inputs may be any that keep to these rules, and one draw needn't show every extreme that they name: `tile_list`: entry 0 is a local source block below 1, entry 1 a local target block below 128; the live slots of a device name distinct pairs; every source block and every target block belongs to some live slot of some device; dead slots hold valid indices. `tile_count`: some device is full in every draw.
All inputs are finite; a program needn't handle non-finite values.
Results may differ from a plain program's by a relative error of at most 0.0003.
Values may be sent and summed in bfloat16 or wider, within the bound.
A program may use at most 64 MiB of HBM per device.

v0:
```python
import jax
import jax.numpy as jnp
from jax import lax
from jax.sharding import PartitionSpec as P

ITERS = 3


EPSILON = 0.5
LOWEST = -1e30


def tile_costs(src_tiles, dst_tiles, src_sq, dst_sq):
    cross = jnp.einsum("tad,tbd->tab", src_tiles, dst_tiles, preferred_element_type=jnp.float32)
    return 0.5 * (src_sq[:, :, None] + dst_sq[:, None, :]) - cross


def block_reduce(maxima, totals, hot_table, occupied):
    masked = jnp.where(hot_table.T[:, :, None] > 0.5, maxima[None, :, :], LOWEST)
    block_max = jnp.max(masked, axis=1)
    slot_max = jnp.dot(hot_table, block_max, precision=lax.Precision.HIGHEST)
    live_col = occupied[:, None]
    weight = jnp.where(
        live_col, totals * jnp.exp(jnp.where(live_col, maxima, slot_max) - slot_max), 0.0
    )
    block_sum = jnp.dot(hot_table.T, weight, precision=lax.Precision.HIGHEST)
    return (block_max, block_sum)


def body(source_points, target_points, source_mass, target_mass, tile_list, tile_count):
    tile_size = source_mass.shape[1]
    row_blocks = source_mass.shape[0]
    col_blocks = target_mass.shape[0]
    feature_dim = source_points.shape[1]
    tile_rows = tile_list[0, 0, 0]
    tile_cols = tile_list[0, 0, 1]
    slot_count = tile_rows.shape[0]
    occupied = jnp.arange(slot_count, dtype=jnp.int32) < tile_count[0, 0]
    row_pick = (tile_rows[:, None] == jnp.arange(row_blocks, dtype=jnp.int32)[None, :]).astype(
        jnp.float32
    )
    col_pick = (tile_cols[:, None] == jnp.arange(col_blocks, dtype=jnp.int32)[None, :]).astype(
        jnp.float32
    )
    row_hot = row_pick * occupied[:, None].astype(jnp.float32)
    col_hot = col_pick * occupied[:, None].astype(jnp.float32)
    gathered = lax.all_gather(target_points, "row", axis=0, tiled=True)
    src_blocks = source_points.reshape(row_blocks, tile_size, feature_dim)
    dst_blocks = gathered.reshape(col_blocks, tile_size, feature_dim)
    src_norms = jnp.einsum(
        "bad,bad->ba", src_blocks, src_blocks, preferred_element_type=jnp.float32
    )
    dst_norms = jnp.einsum(
        "bad,bad->ba", dst_blocks, dst_blocks, preferred_element_type=jnp.float32
    )
    src_tiles = src_blocks[tile_rows]
    dst_tiles = dst_blocks[tile_cols]
    src_sq = jnp.dot(row_pick, src_norms, precision=lax.Precision.HIGHEST)
    dst_sq = jnp.dot(col_pick, dst_norms, precision=lax.Precision.HIGHEST)

    def costs():
        return tile_costs(src_tiles, dst_tiles, src_sq, dst_sq)

    log_source = jnp.log(source_mass)
    log_target = jnp.log(target_mass)
    target_potential = jnp.zeros((col_blocks, tile_size), jnp.float32)
    source_potential = jnp.zeros((row_blocks, tile_size), jnp.float32)
    for iteration in range(ITERS):
        lookup = jnp.dot(col_pick, target_potential, precision=lax.Precision.HIGHEST)
        scores = (lookup[:, None, :] - costs()) / EPSILON
        maxima = jnp.max(scores, axis=2)
        totals = jnp.sum(jnp.exp(scores - maxima[:, :, None]), axis=2)
        block_max, block_sum = block_reduce(maxima, totals, row_hot, occupied)
        whole_max = lax.pmax(block_max, "col")
        block_sum = lax.psum(block_sum * jnp.exp(block_max - whole_max), "col")
        block_max = whole_max
        source_potential = EPSILON * (log_source - block_max - jnp.log(block_sum))
        lookup = jnp.dot(row_pick, source_potential, precision=lax.Precision.HIGHEST)
        scores = (lookup[:, :, None] - costs()) / EPSILON
        maxima = jnp.max(scores, axis=1)
        totals = jnp.sum(jnp.exp(scores - maxima[:, None, :]), axis=1)
        block_max, block_sum = block_reduce(maxima, totals, col_hot, occupied)
        whole_max = lax.pmax(block_max.astype(jnp.bfloat16), "row").astype(block_max.dtype)
        block_sum = lax.psum(block_sum * jnp.exp(block_max - whole_max), "row")
        target_potential = EPSILON * (log_target - whole_max - jnp.log(block_sum))
    return (source_potential, target_potential)


def solution(mesh):
    in_specs = (
        P("row", None),
        P(("col", "row"), None),
        P("row", None),
        P("col", None),
        P("row", "col", None, None),
        P("row", "col"),
    )
    out_specs = (P("row", None), P("col", None))
    return jax.shard_map(body, mesh=mesh, in_specs=in_specs, out_specs=out_specs, check_vma=False)
```

profile of v0, /device:TPU:1, one launch (start us, length us, event | category | flops | bytes accessed | tf_op | source)
XLA Modules:
  0.0 1816.6 jit_solution(1564052314452699418)
XLA Ops:
  7.2 0.7 all-gather.2.cloned.1.call-update
  8.6 0.7 fusion.127
  9.3 0.9 fusion.22
  10.2 0.7 slice_bitcast_fusion
  10.9 0.7 fusion.131
  11.6 0.7 broadcast_compare_fusion
  12.2 0.7 fusion.126
  13.2 141.6 %all-gather.2.cloned.1.call-done = bf16[16384,128]{1,0:T(8,128)(2,1)} async-done(((bf16[256,128]{1,0:T(8,128)(2,1)}), bf16[16384,128]{1,0:T(8,128)(2,1)}) %all-gather.2.cloned.1.call-update) | async-done | bytes 4194320 | tf_op jit(solution)/shard_map/all_gather | solution.py:47
  154.8 4.4 fusion
  159.4 2.9 gather_fusion
  162.3 0.7 fusion.2
  163.0 0.4 exponential_reduce_fusion.5
  163.4 20.5 %pmax.42 = f32[1,128]{1,0:T(1,128)S(1)} all-reduce(f32[1,128]{1,0:T(1,128)S(1)} %bitcast.78), channel_id=1, replica_groups=mesh['row'=64,'col'=8] {'col'}, use_global_device_ids=true, to_apply=%region_2.3 | all-reduce | flops 128 | bytes 1024 | tf_op jit(solution)/shard_map/pmax | solution.py:74
  184.0 0.2 convolution_multiply_fusion.5
  184.2 12.4 psum.42
  196.7 0.4 fusion.3
  197.0 0.7 exponential_reduce_fusion.4
  197.7 0.4 select_reduce_fusion.2
  198.1 0.2 fusion.70
  198.4 221.3 %pmax.43 = bf16[128,128]{1,0:T(8,128)(2,1)S(1)} all-reduce(bf16[128,128]{1,0:T(8,128)(2,1)S(1)} %convert_element_type.57), channel_id=1, replica_groups=mesh['row'=64,'col'=8] {'row'}, use_global_device_ids=true, to_apply=%region_7.8 | all-reduce | flops 16384 | bytes 65536 | tf_op jit(solution)/shard_map/pmax | solution.py:83
  419.6 1.0 convolution_multiply_fusion.2
  420.7 288.3 %all-reduce.4.cloned.1.call-done = f32[128,128]{1,0:T(8,128)} async-done(((f32[128,128]{1,0:T(8,128)}), f32[128,128]{1,0:T(8,128)}) %all-reduce.4.cloned.1.call-update) | async-done | bytes 65552 | tf_op jit(solution)/shard_map/psum | solution.py:84
  709.1 1.0 fusion.11
  710.1 0.4 fusion.4
  710.5 0.4 exponential_reduce_fusion.3
  710.9 22.7 %pmax.44 = f32[1,128]{1,0:T(1,128)S(1)} all-reduce(f32[1,128]{1,0:T(1,128)S(1)} %bitcast.79), channel_id=1, replica_groups=mesh['row'=64,'col'=8] {'col'}, use_global_device_ids=true, to_apply=%region_12.13 | all-reduce | flops 128 | bytes 1024 | tf_op jit(solution)/shard_map/pmax | solution.py:74
  733.6 0.2 convolution_multiply_fusion.4
  733.8 12.4 psum.44
  746.3 0.4 fusion.5
  746.7 0.7 exponential_reduce_fusion.2
  747.3 0.4 select_reduce_fusion.1
  747.7 0.2 fusion.59
  748.0 221.4 %pmax.45 = bf16[128,128]{1,0:T(8,128)(2,1)S(1)} all-reduce(bf16[128,128]{1,0:T(8,128)(2,1)S(1)} %convert_element_type.59), channel_id=1, replica_groups=mesh['row'=64,'col'=8] {'row'}, use_global_device_ids=true, to_apply=%region_17.18 | all-reduce | flops 16384 | bytes 65536 | tf_op jit(solution)/shard_map/pmax | solution.py:83
  969.4 1.0 convolution_multiply_fusion.1
  970.5 288.3 %all-reduce.6.cloned.1.call-done = f32[128,128]{1,0:T(8,128)} async-done(((f32[128,128]{1,0:T(8,128)}), f32[128,128]{1,0:T(8,128)}) %all-reduce.6.cloned.1.call-update) | async-done | bytes 65552 | tf_op jit(solution)/shard_map/psum | solution.py:84
  1258.8 1.0 fusion.16
  1259.8 0.4 fusion.6
  1260.2 0.4 exponential_reduce_fusion.1
  1260.7 22.7 %pmax.46 = f32[1,128]{1,0:T(1,128)S(1)} all-reduce(f32[1,128]{1,0:T(1,128)S(1)} %bitcast.77), channel_id=1, replica_groups=mesh['row'=64,'col'=8] {'col'}, use_global_device_ids=true, to_apply=%region_22.23 | all-reduce | flops 128 | bytes 1024 | tf_op jit(solution)/shard_map/pmax | solution.py:74
  1283.6 12.4 psum.46
  1296.1 0.4 fusion.7
  1296.4 0.7 exponential_reduce_fusion
  1297.1 0.4 select_reduce_fusion
  1297.5 0.2 fusion.48
  1297.7 221.4 %pmax.47 = bf16[128,128]{1,0:T(8,128)(2,1)S(1)} all-reduce(bf16[128,128]{1,0:T(8,128)(2,1)S(1)} %convert_element_type.61), channel_id=1, replica_groups=mesh['row'=64,'col'=8] {'row'}, use_global_device_ids=true, to_apply=%region_27.28 | all-reduce | flops 16384 | bytes 65536 | tf_op jit(solution)/shard_map/pmax | solution.py:83
  1519.1 1.0 convolution_multiply_fusion
  1520.2 288.4 %all-reduce.8.cloned.1.call-done = f32[128,128]{1,0:T(8,128)} async-done(((f32[128,128]{1,0:T(8,128)}), f32[128,128]{1,0:T(8,128)}) %all-reduce.8.cloned.1.call-update) | async-done | bytes 65552 | tf_op jit(solution)/shard_map/psum | solution.py:84
  1808.6 1.5 fusion.20
  (37 shorter events, 1.4 us)
Async XLA Ops:
  7.2 155.1 %copy-start.1 = (bf16[128,128]{1,0:T(8,128)(2,1)S(1)}, bf16[128,128]{1,0:T(8,128)(2,1)}, u32[]{:S(2)}) copy-start(bf16[128,128]{1,0:T(8,128)(2,1)} %param.6) | copy-start | bytes 98308
  7.2 147.6 %all-gather.2.cloned.1.call-start = ((), (), s32[]{:S(2)}) async-start(), calls=%async_computation | async-start | bytes 4259840 | tf_op jit(solution)/shard_map/all_gather | solution.py:47
  7.9 701.1 %all-reduce.4.cloned.1.call-start = ((), (), s32[]{:S(2)}) async-start(), calls=%async_computation.1 | async-start | bytes 131072 | tf_op jit(solution)/shard_map/psum | solution.py:84
  154.8 29.2 %copy-start.4 = (s32[1,1,2,16]{3,2,1,0:T(2,128)S(1)}, s32[1,1,2,16]{3,2,1,0:T(2,128)}, u32[]{:S(2)}) copy-start(s32[1,1,2,16]{3,2,1,0:T(2,128)} %param.10) | copy-start | bytes 388
  154.8 41.8 %copy-start.2 = (f32[1,128]{1,0:T(1,128)S(1)}, f32[1,128]{1,0:T(1,128)}, u32[]{:S(2)}) copy-start(f32[1,128]{1,0:T(1,128)} %param.8) | copy-start | bytes 1540
  159.2 549.8 %copy-start = (f32[128,128]{1,0:T(8,128)S(1)}, f32[128,128]{1,0:T(8,128)}, u32[]{:S(2)}) copy-start(f32[128,128]{1,0:T(8,128)} %param.9) | copy-start | bytes 196612
  420.7 838.1 %all-reduce.6.cloned.1.call-start = ((), (), s32[]{:S(2)}) async-start(), calls=%async_computation.2 | async-start | bytes 131072 | tf_op jit(solution)/shard_map/psum | solution.py:84
  970.4 838.1 %all-reduce.8.cloned.1.call-start = ((), (), s32[]{:S(2)}) async-start(), calls=%async_computation.3 | async-start | bytes 131072 | tf_op jit(solution)/shard_map/psum | solution.py:84
  1296.0 514.1 %copy-start.3 = (f32[1,128]{1,0:T(1,128)}, f32[1,128]{1,0:T(1,128)S(1)}, u32[]{:S(2)}) copy-start(f32[1,128]{1,0:T(1,128)S(1)} %subtract_multiply_fusion.6) | copy-start | bytes 1540
Sparse Core Ops, SparseCore 0:
  11.0 143.7 all-gather.1
  420.8 288.2 all-reduce.3
  970.5 288.2 all-reduce.5
  1520.3 288.2 all-reduce.7
where the time goes:
time: 1830 us; the launch traced here: 1820 us
  waiting for transfers between devices  1010 us (55%)
  blocking collectives  767 us (42%)
    psum x3, waiting for transfers between devices, body(): block_sum = lax.psum(block_sum * jnp.exp(block_max - whole_max), 'row')  865 us
    pmax x3, blocking collectives, body(): lax.pmax(block_max.astype(jnp.bfloat16), 'row').astype(block_max.dtype)  664 us
    all_gather x1, waiting for transfers between devices, body(): gathered = lax.all_gather(target_points, 'row', axis=0, tiled=True)  142 us
    pmax x3, blocking collectives, body(): whole_max = lax.pmax(block_max, 'col')  65.9 us
    psum x3, blocking collectives, body(): block_sum = lax.psum(block_sum * jnp.exp(block_max - whole_max), 'col')  37.2 us
  transfers between devices with their start and end apart: 4, of which 4 were waited for; matrix products, arithmetic and copies ran while one was open for 0% of the time, Pallas kernels for 0%

commit v1 on v0

v1 whole, which is shorter than its diff:
```python
import functools
import math

import jax
import jax.numpy as jnp
from jax import lax
from jax.experimental import pallas as pl
from jax.experimental.pallas import tpu as pltpu
from jax.sharding import PartitionSpec as P

ITERS = 3
EPSILON = 0.5
LOWEST = -1e30
SCALE = math.log2(math.e) / EPSILON
TILE = 128
OWN = 2
MESH = pl.DeviceIdType.MESH


def far_first(count):
    return sorted(range(1, count), key=lambda d: (-min(d, count - d), d))


def half_norms(points):
    wide = points.astype(jnp.float32)
    square = wide * wide
    high = square.astype(jnp.bfloat16)
    low = (square - high.astype(jnp.float32)).astype(jnp.bfloat16)
    ones = jnp.ones((8, points.shape[1]), jnp.bfloat16)
    total = cross(ones, high) + cross(ones, low)
    return total[0:1] * (0.5 * SCALE)


def cross(left, right):
    return lax.dot_general(
        left, right, (((1,), (1,)), ((), ())), preferred_element_type=jnp.float32
    )


def merge(parts):
    top = jnp.max(parts, axis=0)
    return top + jnp.log2(jnp.sum(jnp.exp2(parts - top[None]), axis=0))


def kernel(
    dims,
    src_ref,
    tgt_ref,
    smass_ref,
    tmass_ref,
    list_ref,
    count_ref,
    osrc_ref,
    otgt_ref,
    full,
    tall,
    meta,
    bias,
    ts_score,
    st_score,
    columns,
    s_top,
    s_sum,
    t_top,
    t_sum,
    lbuf,
    rbuf,
    zbuf,
    qbuf,
    ybuf,
    obuf,
    first_send,
    first_recv,
    iter_send,
    iter_recv,
):
    ny, nz, nx, nk = dims
    owners = nx * nk
    blocks = OWN * ny
    row, col = lax.axis_index("row"), lax.axis_index("col")
    y, z = lax.div(row, nz), lax.rem(row, nz)
    x, k = lax.div(col, nk), lax.rem(col, nk)

    def at_y(d):
        return (lax.rem(y + d, ny) * nz + z, col)

    def at_z(d):
        return (y * nz + lax.rem(z + d, nz), col)

    def at_x(d):
        return (row, lax.rem(x + d, nx) * nk + k)

    def at_k(d):
        return (row, x * nk + lax.rem(k + d, nk))

    def at_col(d):
        return (row, lax.rem(col + d, owners))

    def send(src, dst, sems, where):
        pltpu.make_async_remote_copy(
            src_ref=src,
            dst_ref=dst,
            send_sem=sems[0],
            recv_sem=sems[1],
            device_id=where,
            device_id_type=MESH,
        ).start()

    def settle(ref, sem):
        pltpu.make_async_copy(ref, ref, sem).wait()

    barrier = pltpu.get_barrier_semaphore()
    partners = (
        [at_z(d) for d in far_first(nz)]
        + [at_y(d) for d in far_first(ny)]
        + [at_col(d) for d in far_first(owners)]
    )
    for where in partners:
        pl.semaphore_signal(barrier, inc=1, device_id=where, device_id_type=MESH)

    lane = lax.broadcasted_iota(jnp.int32, (1, TILE), 1)
    count = count_ref[0, 0]
    live = jnp.zeros((1, TILE), jnp.float32)
    for slot in range(list_ref.shape[3]):
        block = jnp.where(slot < count, list_ref[0, 0, 1, slot], -1)
        live = jnp.where(lane == block, 1.0, live)
    meta[z, :, 0:TILE] = jnp.where(live > 0.5, 0.0, LOWEST)
    meta[z, :, TILE : 2 * TILE] = jnp.log2(smass_ref[...])
    part = TILE // owners
    full[z, x, k] = src_ref[pl.ds(pl.multiple_of(col * part, part), part), :]
    tall[y] = tgt_ref[...]

    pl.semaphore_wait(barrier, len(partners))

    def sems(stage):
        return first_send.at[stage], first_recv.at[stage]

    for d in far_first(nz):
        send(meta.at[z], meta.at[z], sems(0), at_z(d))
        send(full.at[z, x, k], full.at[z, x, k], sems(1), at_z(d))
    for d in far_first(ny):
        send(tall.at[y], tall.at[y], sems(2), at_y(d))
    settle(full.at[0 : nz - 1, 0, 0], first_recv.at[1])
    for d in far_first(nx):
        send(full.at[:, x, k], full.at[:, x, k], sems(3), at_x(d))
    if nx > 1:
        settle(full.at[:, 0 : nx - 1, 0], first_recv.at[3])
    for d in far_first(nk):
        send(full.at[:, :, k], full.at[:, :, k], sems(4), at_k(d))

    settle(meta.at[0 : nz - 1], first_recv.at[0])
    drop = meta[:, 0, 0:TILE]
    for tb in range(blocks):
        mine = OWN * nz * (tb // OWN) + OWN * z + tb % OWN
        picked = jnp.sum(jnp.where(lane == mine, drop, 0.0), axis=1, keepdims=True)
        bias[tb] = jnp.broadcast_to(picked, (nz, TILE))
    settle(tall.at[0 : ny - 1], first_recv.at[2])
    half = [
        half_norms(tall[tb // OWN, (tb % OWN) * TILE : (tb % OWN + 1) * TILE, :])
        for tb in range(blocks)
    ]
    tgt_half = jnp.concatenate(half, axis=0)
    src_half = half_norms(src_ref[...])
    src_log = meta[pl.ds(OWN * col, OWN), :, TILE : 2 * TILE]
    tgt_log = jnp.log2(
        jnp.concatenate(
            [tmass_ref[pl.ds(OWN * nz * yy + OWN * z, OWN), :] for yy in range(ny)], axis=0
        )
    )
    if nk > 1:
        settle(full.at[:, :, 0 : nk - 1], first_recv.at[4])

    def build(zz, carry):
        source = full[zz].reshape(TILE, TILE)
        for tb in range(blocks):
            target = tall[tb // OWN, (tb % OWN) * TILE : (tb % OWN + 1) * TILE, :]
            off = bias[tb, pl.ds(zz, 1), :]
            ts_score[zz, tb * TILE : (tb + 1) * TILE, :] = cross(target, source) * SCALE + off
            rows = pl.ds(pl.multiple_of(zz * TILE, TILE), TILE)
            st_score[tb, rows, :] = cross(source, target) * SCALE + off
        return carry

    lax.fori_loop(0, nz, build, 0)

    def stand(rows):
        turned = jnp.transpose(rows)
        for b in range(rows.shape[0]):
            columns[b * TILE : (b + 1) * TILE, :] = jnp.broadcast_to(
                turned[:, b : b + 1], (TILE, TILE)
            )

    def reduce(score, tops, sums, outer, inner):
        def step(b, carry):
            for i in range(inner):
                at = slice(i * TILE, (i + 1) * TILE)
                s = (score[b, at, :] + columns[at, :]).reshape(TILE // 8, 8, TILE)
                top = jnp.max(s, axis=0)
                tops[b, i * 8 : (i + 1) * 8, :] = top
                sums[b, i * 8 : (i + 1) * 8, :] = jnp.sum(jnp.exp2(s - top[None]), axis=0)
            return carry

        lax.fori_loop(0, outer, step, 0)
        top = jnp.max(tops[...], axis=1)
        total = jnp.sum(jnp.exp2(tops[...] - top[:, None, :]) * sums[...], axis=1)
        return top + jnp.log2(total)

    def pair(it, stage):
        return iter_send.at[it, stage], iter_recv.at[it, stage]

    tgt_pot = -tgt_half
    for it in range(ITERS):
        stand(tgt_pot)
        part_sum = reduce(ts_score, s_top, s_sum, nz, blocks)
        for b in range(nz):
            lbuf[it, b] = part_sum[b : b + 1, :]
        for d in far_first(owners):
            other = lax.rem(col + d, owners)
            send(
                lbuf.at[it, pl.ds(OWN * other, OWN)], rbuf.at[it, col], pair(it, 0), at_col(d)
            )
        rbuf[it, col] = lbuf[it, pl.ds(OWN * col, OWN)]
        settle(rbuf.at[it, 0 : owners - 1], iter_recv.at[it, 0])
        zbuf[it, z] = merge(rbuf[it])
        for d in far_first(nz):
            send(zbuf.at[it, z], zbuf.at[it, z], pair(it, 1), at_z(d))
        settle(zbuf.at[it, 0 : nz - 1], iter_recv.at[it, 1])
        qbuf[it, pl.ds(OWN * col, OWN)] = src_log - merge(zbuf[it])
        for d in far_first(owners):
            mine = qbuf.at[it, pl.ds(OWN * col, OWN)]
            send(mine, mine, pair(it, 2), at_col(d))
        settle(qbuf.at[it, 0 : nz - OWN], iter_recv.at[it, 2])
        stand(qbuf[it, :, 0, :])
        ybuf[it, y] = reduce(st_score, t_top, t_sum, blocks, nz)
        for d in far_first(ny):
            send(ybuf.at[it, y], ybuf.at[it, y], pair(it, 3), at_y(d))
        settle(ybuf.at[it, 0 : ny - 1], iter_recv.at[it, 3])
        tgt_pot = tgt_log - merge(ybuf[it])

    obuf[z] = (tgt_pot + tgt_half) * (1.0 / SCALE)
    for d in far_first(nz):
        send(obuf.at[z], obuf.at[z], sems(5), at_z(d))
    osrc_ref[...] = (qbuf[ITERS - 1, z] + src_half) * (1.0 / SCALE)

    settle(meta.at[0 : nz - 1], first_send.at[0])
    settle(full.at[0 : nz - 1, 0, 0], first_send.at[1])
    settle(tall.at[0 : ny - 1], first_send.at[2])
    if nx > 1:
        settle(full.at[:, 0 : nx - 1, 0], first_send.at[3])
    if nk > 1:
        settle(full.at[:, :, 0 : nk - 1], first_send.at[4])
    for it in range(ITERS):
        settle(rbuf.at[it, 0 : owners - 1], iter_send.at[it, 0])
        settle(zbuf.at[it, 0 : nz - 1], iter_send.at[it, 1])
        settle(qbuf.at[it, 0 : nz - OWN], iter_send.at[it, 2])
        settle(ybuf.at[it, 0 : ny - 1], iter_send.at[it, 3])
    settle(obuf.at[0 : nz - 1], first_recv.at[5])
    settle(obuf.at[0 : nz - 1], first_send.at[5])
    for zz in range(nz):
        for yy in range(ny):
            at = OWN * (yy * nz + zz)
            otgt_ref[at : at + OWN, :] = obuf[zz, OWN * yy : OWN * (yy + 1), :]


def body(dims, *args):
    ny, nz, nx, nk = dims
    owners = nx * nk
    blocks = OWN * ny
    vmem = pl.BlockSpec(memory_space=pltpu.VMEM)
    smem = pl.BlockSpec(memory_space=pltpu.SMEM)
    f32 = jnp.float32
    return pl.pallas_call(
        functools.partial(kernel, dims),
        out_shape=(
            jax.ShapeDtypeStruct((1, TILE), f32),
            jax.ShapeDtypeStruct((blocks * nz, TILE), f32),
        ),
        in_specs=[vmem, vmem, vmem, vmem, smem, smem],
        out_specs=(vmem, vmem),
        scratch_shapes=[
            pltpu.VMEM((nz, nx, nk, TILE // owners, TILE), jnp.bfloat16),
            pltpu.VMEM((ny, OWN * TILE, TILE), jnp.bfloat16),
            pltpu.VMEM((nz, 1, 2 * TILE), f32),
            pltpu.VMEM((blocks, nz, TILE), f32),
            pltpu.VMEM((nz, blocks * TILE, TILE), f32),
            pltpu.VMEM((blocks, nz * TILE, TILE), f32),
            pltpu.VMEM((max(nz, blocks) * TILE, TILE), f32),
            pltpu.VMEM((nz, blocks * 8, TILE), f32),
            pltpu.VMEM((nz, blocks * 8, TILE), f32),
            pltpu.VMEM((blocks, nz * 8, TILE), f32),
            pltpu.VMEM((blocks, nz * 8, TILE), f32),
            pltpu.VMEM((ITERS, nz, 1, TILE), f32),
            pltpu.VMEM((ITERS, owners, OWN, 1, TILE), f32),
            pltpu.VMEM((ITERS, nz, OWN, 1, TILE), f32),
            pltpu.VMEM((ITERS, nz, 1, TILE), f32),
            pltpu.VMEM((ITERS, ny, blocks, TILE), f32),
            pltpu.VMEM((nz, blocks, TILE), f32),
            pltpu.SemaphoreType.DMA((6,)),
            pltpu.SemaphoreType.DMA((6,)),
            pltpu.SemaphoreType.DMA((ITERS, 4)),
            pltpu.SemaphoreType.DMA((ITERS, 4)),
        ],
        compiler_params=pltpu.CompilerParams(
            collective_id=0, has_side_effects=True, vmem_limit_bytes=40 * 2**20
        ),
    )(*args)


def solution(mesh, dims=(4, 16, 4, 2)):
    in_specs = (
        P("row", None),
        P(("col", "row"), None),
        P("row", None),
        P("col", None),
        P("row", "col", None, None),
        P("row", "col"),
    )
    out_specs = (P("row", None), P("col", None))
    return jax.shard_map(
        functools.partial(body, dims),
        mesh=mesh,
        in_specs=in_specs,
        out_specs=out_specs,
        check_vma=False,
    )
```

time: 1830 us -> 113 us (0.06)
  waiting for transfers between devices: 1010 us -> 0 us
  blocking collectives: 767 us -> 0 us
  Pallas kernels: 0 us -> 107 us
    psum x3 -> x0, waiting for transfers between devices: 865 us -> none  [body(): block_sum = lax.psum(block_sum * jnp.exp(block_max - whole_max), 'row')]
    pmax x6 -> x0, blocking collectives: 730 us -> none  [the longest x3 664 us: body(): lax.pmax(block_max.astype(jnp.bfloat16), 'row').astype(block_max.dtype)]
    all_gather x1 -> x0, waiting for transfers between devices: 142 us -> none  [body(): gathered = lax.all_gather(target_points, 'row', axis=0, tiled=True)]
    pallas_call x0 -> x1, Pallas kernels: none -> 107 us  [body(): pl.pallas_call(functools.partial(kernel, dims), out_shape=(jax.ShapeDtype...]
    psum x3 -> x0, blocking collectives: 37.2 us -> none  [body(): block_sum = lax.psum(block_sum * jnp.exp(block_max - whole_max), 'col')]
  transfers between devices with their start and end apart: 4 -> 0, of which waited for: 4 -> 0; matrix products, arithmetic and copies ran while one was open for 0% -> 0% of each run, Pallas kernels for 0% -> 0%
where the time goes in v1:
time: 113 us; the launch traced here: 112 us
  Pallas kernels  107 us (95%)
  local copies, waits for them, and re-layouts  3.58 us (3%)
  between operations  1.35 us (1%)
    pallas_call x1, Pallas kernels, body(): pl.pallas_call(functools.partial(kernel, dims), out_shape=(jax.ShapeDtype...  107 us
    unnamed x12, local copies, waits for them, and re-layouts  3.58 us

profile of v1, /device:TPU:1, one launch (start us, length us, event | category | flops | bytes accessed | tf_op | source)
XLA Modules:
  0.0 112.4 jit_solution(17744963505427702691)
XLA Ops:
  0.6 0.0 copy-start.3
  0.6 0.0 copy-start.4
  1.3 0.0 copy-done.3
  1.3 0.0 copy-done.4
  1.3 0.0 copy-start
  1.3 0.8 copy-done
  2.2 0.0 copy-start.1
  2.2 0.8 copy-done.1
  3.0 0.0 copy-start.2
  3.0 0.8 copy-done.2
  3.8 107.4 %shard_map.77 = (f32[1,128]{1,0:T(1,128)S(1)}, f32[128,128]{1,0:T(8,128)S(1)}) custom-call(bf16[128,128]{1,0:T(8,128)(2,1)S(1)} %copy-done.2, bf16[256,128]{1,0:T(8,128)(2,1)S(1)} %copy-done, f32[1,128]{1,0:T(1,128)S(1)} %copy-done.4, f32[128,128]{1,0:T(8,128)S(1)} %copy-done.1, s32[1,1,2,16]{3,2,1,0:T(2,128)S(1)} %copy-done.3, s32[1,1]{1,0:T(1,128)S(6)} %copy.10.count_ref), custom_call_target="tpu_custom_call" | custom-call | tf_op jit(solution)/shard_map/pallas_call | solution.py:271
  111.2 0.5 copy.11
  111.7 0.6 copy.12
Async XLA Ops:
  0.6 0.7 copy-start.3
  0.6 0.7 copy-start.4
  1.3 0.8 copy-start
  2.2 0.8 copy-start.1
  3.0 0.8 copy-start.2

commit v2 on v1

v2 whole, which is shorter than its diff:
```python
import functools
import math

import jax
import jax.numpy as jnp
from jax import lax
from jax.experimental import pallas as pl
from jax.experimental.pallas import tpu as pltpu
from jax.sharding import PartitionSpec as P

ITERS = 3
EPSILON = 0.5
LOWEST = -1e30
SCALE = math.log2(math.e) / EPSILON
TILE = 128
OWN = 2
MESH = pl.DeviceIdType.MESH


def far_first(count):
    return sorted(range(1, count), key=lambda d: (-min(d, count - d), d))


def cross(left, right):
    return lax.dot_general(
        left, right, (((1,), (1,)), ((), ())), preferred_element_type=jnp.float32
    )


def half_norms(points):
    wide = points.astype(jnp.float32)
    square = wide * wide
    high = square.astype(jnp.bfloat16)
    low = (square - high.astype(jnp.float32)).astype(jnp.bfloat16)
    ones = jnp.ones((8, points.shape[1]), jnp.bfloat16)
    total = cross(ones, high) + cross(ones, low)
    return total[0:1] * (0.5 * SCALE)


def merge(parts):
    top = jnp.max(parts, axis=0)
    return top + jnp.log2(jnp.sum(jnp.exp2(parts - top[None]), axis=0))


def fold(s):
    s = s.reshape(s.shape[0] // 8, 8, TILE)
    top = jnp.max(s, axis=0)
    return top, jnp.sum(jnp.exp2(s - top[None]), axis=0)


def close(tops, sums):
    top = jnp.max(tops, axis=1)
    total = jnp.sum(jnp.exp2(tops - top[:, None, :]) * sums, axis=1)
    return top + jnp.log2(total)


def kernel(
    dims,
    src_hbm,
    tgt_hbm,
    smass_hbm,
    tmass_hbm,
    list_hbm,
    count_hbm,
    osrc_ref,
    otgt_ref,
    src,
    tmass,
    smass,
    slots,
    count,
    full,
    tall,
    own,
    meta,
    hold,
    logs,
    bias,
    ts_score,
    st_score,
    columns,
    s_top,
    s_sum,
    t_top,
    t_sum,
    xbuf,
    zbuf,
    ybuf,
    qrow,
    sib,
    pots,
    obuf,
    local_sem,
    piece_sem,
    first_send,
    first_recv,
    iter_send,
    iter_recv,
):
    ny, nz, nx, nk = dims
    group = ny * nk
    held = nz // nk
    blocks = OWN * group
    part = TILE // nx
    row, col = lax.axis_index("row"), lax.axis_index("col")
    y, z = lax.div(row, nz), lax.rem(row, nz)
    x, k = lax.div(col, nk), lax.rem(col, nk)
    seat = y * nk + k
    mine = lax.div(z, nk)
    shift = lax.rem(k + nz - lax.rem(z, nk), nk)

    def at_z(d):
        return (y * nz + lax.rem(z + d, nz), col)

    def at_x(d):
        return (row, lax.rem(x + d, nx) * nk + k)

    def at_k(d):
        return (row, x * nk + lax.rem(k + d, nk))

    def at_seat(d):
        other = lax.rem(seat + d, group)
        return (lax.div(other, nk) * nz + z, x * nk + lax.rem(other, nk))

    def send(src_ref, dst_ref, sems, where):
        pltpu.make_async_remote_copy(
            src_ref=src_ref,
            dst_ref=dst_ref,
            send_sem=sems[0],
            recv_sem=sems[1],
            device_id=where,
            device_id_type=MESH,
        ).start()

    def settle(ref, sem):
        pltpu.make_async_copy(ref, ref, sem).wait()

    loads = [
        pltpu.make_async_copy(src_hbm, src, local_sem.at[0]),
        pltpu.make_async_copy(tgt_hbm, tall.at[seat], local_sem.at[1]),
        pltpu.make_async_copy(smass_hbm, smass, local_sem.at[2]),
        pltpu.make_async_copy(tmass_hbm, tmass, local_sem.at[3]),
        pltpu.make_async_copy(list_hbm, slots, local_sem.at[4]),
        pltpu.make_async_copy(count_hbm, count, local_sem.at[5]),
    ]
    for load in loads:
        load.start()

    barrier = pltpu.get_barrier_semaphore()
    partners = (
        [at_z(d) for d in far_first(nz)]
        + [at_seat(d) for d in range(1, group)]
        + [at_x(d) for d in far_first(nx)]
    )
    for where in partners:
        pl.semaphore_signal(barrier, inc=1, device_id=where, device_id_type=MESH)
    for load in loads:
        load.wait()

    lane = lax.broadcasted_iota(jnp.int32, (1, TILE), 1)
    used = count[0, 0]
    live = jnp.zeros((1, TILE), jnp.float32)
    for slot in range(slots.shape[3]):
        block = jnp.where(slot < used, slots[0, 0, 1, slot], -1)
        live = jnp.where(lane == block, 1.0, live)
    own[0, :, 0:TILE] = jnp.where(live > 0.5, 0.0, LOWEST)
    own[0, :, TILE : 2 * TILE] = jnp.log2(smass[...])
    for yy in range(ny):
        at = OWN * nz * yy + OWN * z
        logs[yy, k] = jnp.log2(tmass[pl.ds(at, OWN), :])

    pl.semaphore_wait(barrier, len(partners))

    def sems(stage):
        return first_send.at[stage], first_recv.at[stage]

    my_slot = full.at[mine * nx + x]
    my_part = src.at[pl.ds(pl.multiple_of(x * part, part), part)]

    @pl.when(shift == 0)
    def _():
        for d in far_first(nz):
            send(my_part, my_slot, (first_send.at[0], piece_sem.at[0, mine]), at_z(d))
        pltpu.make_async_copy(my_part, my_slot, piece_sem.at[0, mine]).start()

    @pl.when(shift != 0)
    def _():
        send(own.at[0], meta.at[mine, k], sems(1), at_k(1))

    for d in range(1, group):
        send(tall.at[seat], tall.at[seat], sems(3), at_seat(d))
    send(logs.at[:, k], logs.at[:, k], sems(4), at_k(1))

    @pl.when(shift == 0)
    def _():
        meta[mine, k] = own[0]
        settle(own.at[0], first_recv.at[1])
        for d in far_first(nz):
            send(meta.at[mine], meta.at[mine], sems(2), at_z(d))

    def slot_at(i):
        odd = lax.rem(i, 2)
        m = odd * lax.div(i + 1, 2) + (1 - odd) * lax.rem(held - lax.div(i, 2), held)
        return lax.div(lax.rem(z + shift + nk * m, nz), nk)

    def forward(i, carry):
        j = slot_at(i)
        settle(full.at[j * nx + x], piece_sem.at[0, j])
        for d in far_first(nx):
            piece = full.at[j * nx + x]
            send(piece, piece, (first_send.at[5], piece_sem.at[1, j]), at_x(d))
        return carry

    lax.fori_loop(0, held, forward, 0)

    def targets(tb):
        at = tb % OWN * TILE
        return tall[tb // OWN, at : at + TILE, :]

    settle(tall.at[0 : group - 1], first_recv.at[3])
    tgt_half = jnp.concatenate([half_norms(targets(tb)) for tb in range(blocks)], axis=0)
    src_half = half_norms(src[...])

    @pl.when(shift == 0)
    def _():
        settle(meta.at[0 : held - 1], first_recv.at[2])

    @pl.when(shift != 0)
    def _():
        settle(meta, first_recv.at[2])

    for tb in range(blocks):
        drop = meta[:, tb // OWN % nk, 0, 0:TILE]
        at = OWN * nz * (tb // OWN // nk) + OWN * z + tb % OWN
        picked = jnp.sum(jnp.where(lane == at, drop, 0.0), axis=1, keepdims=True)
        bias[tb] = jnp.broadcast_to(picked, (held, TILE))
    src_log = meta[:, 0, 0, TILE : 2 * TILE]
    settle(logs.at[:, 0], first_recv.at[4])
    tgt_log = jnp.concatenate(
        [logs[i // nk, i % nk] for i in range(group)], axis=0
    )

    def stand(rows):
        turned = jnp.transpose(rows)
        for b in range(rows.shape[0]):
            columns[b * TILE : (b + 1) * TILE, :] = jnp.broadcast_to(
                turned[:, b : b + 1], (TILE, TILE)
            )

    def first_half(i, carry):
        j = slot_at(i)
        if nx > 1:
            settle(full.at[pl.ds(j * nx, nx - 1)], piece_sem.at[1, j])
        source = full[pl.ds(j * nx, nx)].reshape(TILE, TILE)
        for tb in range(blocks):
            at = slice(tb * TILE, (tb + 1) * TILE)
            tile = cross(targets(tb), source) * SCALE + bias[tb, pl.ds(j, 1), :]
            ts_score[j, at, :] = tile
            top, total = fold(tile + columns[at, :])
            s_top[j, tb * 8 : (tb + 1) * 8, :] = top
            s_sum[j, tb * 8 : (tb + 1) * 8, :] = total
        return carry

    def source_half(j, carry):
        for tb in range(blocks):
            at = slice(tb * TILE, (tb + 1) * TILE)
            top, total = fold(ts_score[j, at, :] + columns[at, :])
            s_top[j, tb * 8 : (tb + 1) * 8, :] = top
            s_sum[j, tb * 8 : (tb + 1) * 8, :] = total
        return carry

    def build(j, carry):
        source = full[pl.ds(j * nx, nx)].reshape(TILE, TILE)
        rows = pl.ds(pl.multiple_of(j * TILE, TILE), TILE)
        for tb in range(blocks):
            st_score[tb, rows, :] = cross(source, targets(tb)) * SCALE + bias[tb, pl.ds(j, 1), :]
        return carry

    def target_half(tb, carry):
        for j in range(held):
            at = slice(j * TILE, (j + 1) * TILE)
            top, total = fold(st_score[tb, at, :] + columns[at, :])
            t_top[tb, j * 8 : (j + 1) * 8, :] = top
            t_sum[tb, j * 8 : (j + 1) * 8, :] = total
        return carry

    def pair(it, stage):
        return iter_send.at[it, stage], iter_recv.at[it, stage]

    tgt_pot = -tgt_half
    for it in range(ITERS):
        stand(tgt_pot)
        lax.fori_loop(0, held, source_half if it else first_half, 0)
        xbuf[it, x] = close(s_top[...], s_sum[...])
        for d in far_first(nx):
            send(xbuf.at[it, x], xbuf.at[it, x], pair(it, 0), at_x(d))
        if nx > 1:
            settle(xbuf.at[it, 0 : nx - 1], iter_recv.at[it, 0])
        zbuf[it, z] = merge(xbuf[it])
        for d in far_first(nz):
            send(zbuf.at[it, z], zbuf.at[it, z], pair(it, 1), at_z(d))
        if it == 0:
            lax.fori_loop(0, held, build, 0)
        settle(zbuf.at[it, 0 : nz - 1], iter_recv.at[it, 1])
        src_pot = src_log - merge(zbuf[it])
        stand(src_pot)
        if it == ITERS - 1:
            for j in range(held):
                qrow[j] = src_pot[j : j + 1, :]

            @pl.when(shift == 0)
            def _():
                sib[0] = qrow[mine]
                send(sib.at[0], sib.at[1], sems(6), at_k(1))

        lax.fori_loop(0, blocks, target_half, 0)
        ybuf[it, seat] = close(t_top[...], t_sum[...])
        for d in range(1, group):
            send(ybuf.at[it, seat], ybuf.at[it, seat], pair(it, 2), at_seat(d))
        settle(ybuf.at[it, 0 : group - 1], iter_recv.at[it, 2])
        tgt_pot = tgt_log - merge(ybuf[it])

    result = (tgt_pot + tgt_half) * (1.0 / SCALE)
    for i in range(group):
        pots[i] = result[OWN * i : OWN * (i + 1), :]
    for yy in range(ny):
        obuf[z, yy] = pots[yy * nk + k]
    for d in far_first(nz):
        send(obuf.at[z], obuf.at[z], sems(7), at_z(d))

    @pl.when(shift == 0)
    def _():
        osrc_ref[...] = (sib[0] + src_half) * (1.0 / SCALE)
        settle(sib.at[0], first_send.at[6])
        settle(full.at[0 : nz - 1], first_send.at[0])
        settle(hold, first_send.at[2])

    @pl.when(shift != 0)
    def _():
        settle(sib.at[1], first_recv.at[6])
        osrc_ref[...] = (sib[1] + src_half) * (1.0 / SCALE)
        settle(own.at[0], first_send.at[1])

    settle(tall.at[0 : group - 1], first_send.at[3])
    settle(logs.at[:, 0], first_send.at[4])
    if nx > 1:
        settle(full.at[0 : held * (nx - 1)], first_send.at[5])
    for it in range(ITERS):
        if nx > 1:
            settle(xbuf.at[it, 0 : nx - 1], iter_send.at[it, 0])
        settle(zbuf.at[it, 0 : nz - 1], iter_send.at[it, 1])
        settle(ybuf.at[it, 0 : group - 1], iter_send.at[it, 2])
    settle(obuf.at[0 : nz - 1], first_recv.at[7])
    settle(obuf.at[0 : nz - 1], first_send.at[7])
    for zz in range(nz):
        for yy in range(ny):
            at = OWN * (yy * nz + zz)
            otgt_ref[at : at + OWN, :] = obuf[zz, yy]


def body(dims, *args):
    ny, nz, nx, nk = dims
    group = ny * nk
    held = nz // nk
    blocks = OWN * group
    f32, bf16 = jnp.float32, jnp.bfloat16
    dma = pltpu.SemaphoreType.DMA
    return pl.pallas_call(
        functools.partial(kernel, dims),
        out_shape=(
            jax.ShapeDtypeStruct((1, TILE), f32),
            jax.ShapeDtypeStruct((OWN * ny * nz, TILE), f32),
        ),
        in_specs=[pl.BlockSpec(memory_space=pl.ANY)] * 6,
        out_specs=(pl.BlockSpec(memory_space=pltpu.VMEM),) * 2,
        scratch_shapes=[
            pltpu.VMEM(args[0].shape, bf16),
            pltpu.VMEM(args[3].shape, f32),
            pltpu.VMEM(args[2].shape, f32),
            pltpu.SMEM(args[4].shape, jnp.int32),
            pltpu.SMEM(args[5].shape, jnp.int32),
            pltpu.VMEM((held * nx, TILE // nx, TILE), bf16),
            pltpu.VMEM((group, OWN * TILE, TILE), bf16),
            pltpu.VMEM((1, 1, 2 * TILE), f32),
            pltpu.VMEM((held, nk, 1, 2 * TILE), f32),
            pltpu.VMEM((nz - 1, nk, 1, 2 * TILE), f32),
            pltpu.VMEM((ny, nk, OWN, TILE), f32),
            pltpu.VMEM((blocks, held, TILE), f32),
            pltpu.VMEM((held, blocks * TILE, TILE), f32),
            pltpu.VMEM((blocks, held * TILE, TILE), f32),
            pltpu.VMEM((max(held, blocks) * TILE, TILE), f32),
            pltpu.VMEM((held, blocks * 8, TILE), f32),
            pltpu.VMEM((held, blocks * 8, TILE), f32),
            pltpu.VMEM((blocks, held * 8, TILE), f32),
            pltpu.VMEM((blocks, held * 8, TILE), f32),
            pltpu.VMEM((ITERS, nx, held, TILE), f32),
            pltpu.VMEM((ITERS, nz, held, TILE), f32),
            pltpu.VMEM((ITERS, group, blocks, TILE), f32),
            pltpu.VMEM((held, 1, TILE), f32),
            pltpu.VMEM((2, 1, TILE), f32),
            pltpu.VMEM((group, OWN, TILE), f32),
            pltpu.VMEM((nz, ny, OWN, TILE), f32),
            dma((6,)),
            dma((2, held)),
            dma((8,)),
            dma((8,)),
            dma((ITERS, 3)),
            dma((ITERS, 3)),
        ],
        compiler_params=pltpu.CompilerParams(
            collective_id=0, has_side_effects=True, vmem_limit_bytes=56 * 2**20
        ),
    )(*args)


def solution(mesh, dims=(4, 16, 4, 2)):
    in_specs = (
        P("row", None),
        P(("col", "row"), None),
        P("row", None),
        P("col", None),
        P("row", "col", None, None),
        P("row", "col"),
    )
    out_specs = (P("row", None), P("col", None))
    return jax.shard_map(
        functools.partial(body, dims),
        mesh=mesh,
        in_specs=in_specs,
        out_specs=out_specs,
        check_vma=False,
    )
```

time: 113 us -> 96.4 us (0.85)
  Pallas kernels: 107 us -> 92.3 us
    pallas_call x1, Pallas kernels: 107 us -> 92.3 us  [body(): pl.pallas_call(functools.partial(kernel, dims), out_shape=(jax.ShapeDtype...]
    unnamed x12 -> x4, local copies, waits for them, and re-layouts: 3.58 us -> 2.57 us
where the time goes in v2:
time: 96.4 us; the launch traced here: 96.1 us
  Pallas kernels  92.3 us (96%)
  local copies, waits for them, and re-layouts  2.57 us (3%)
  between operations  1.29 us (1%)
    pallas_call x1, Pallas kernels, body(): pl.pallas_call(functools.partial(kernel, dims), out_shape=(jax.ShapeDtype...  92.3 us
    unnamed x4, local copies, waits for them, and re-layouts  2.57 us

profile of v2, /device:TPU:1, one launch (start us, length us, event | category | flops | bytes accessed | tf_op | source)
XLA Modules:
  0.0 96.1 jit_solution(7568604062828679760)
XLA Ops:
  1.3 92.3 %shard_map.77 = (f32[1,128]{1,0:T(1,128)}, f32[128,128]{1,0:T(8,128)}) custom-call(bf16[128,128]{1,0:T(8,128)(2,1)} %src_hbm.1, bf16[256,128]{1,0:T(8,128)(2,1)} %tgt_hbm.1, f32[1,128]{1,0:T(1,128)} %smass_hbm.1, f32[128,128]{1,0:T(8,128)} %tmass_hbm.1, s32[1,1,2,16]{3,2,1,0:T(2,128)} %list_hbm.1, s32[1,1]{1,0:T(1,128)S(6)} %copy.10.count_hbm), custom_call_target="tpu_custom_call" | custom-call | tf_op jit(solution)/shard_map/pallas_call | solution.py:368
  93.5 0.0 copy-start
  93.5 0.6 copy-done
  94.1 0.5 copy.11
  94.6 1.5 %copy.12 = f32[128,128]{1,0:T(8,128)} copy(f32[128,128]{1,0:T(8,128)} %get-tuple-element.5) | data formatting | bytes 131072
Async XLA Ops:
  93.5 0.6 copy-start

commit v3 on v2

--- a/solution.py
+++ b/solution.py
@@ -75,6 +75,9 @@
     meta,
     hold,
     logs,
+    halves,
+    picks_src,
+    picks_tgt,
     bias,
     ts_score,
     st_score,
@@ -157,6 +160,15 @@
     for load in loads:
         load.wait()
 
+    for picks in (picks_src, picks_tgt):
+        n = picks.shape[0] // 3
+        which = lax.rem(lax.broadcasted_iota(jnp.int32, picks.shape, 0), n)
+        place = lax.div(lax.broadcasted_iota(jnp.int32, picks.shape, 1), TILE)
+        picks[...] = jnp.where(which == place, 1.0, 0.0).astype(jnp.bfloat16)
+    own_half = half_norms(tall[seat])
+    for i in range(OWN):
+        halves[seat, i : i + 1, :] = own_half[:, i * TILE : (i + 1) * TILE]
+    src_half = half_norms(src[...])
     lane = lax.broadcasted_iota(jnp.int32, (1, TILE), 1)
     used = count[0, 0]
     live = jnp.zeros((1, TILE), jnp.float32)
@@ -188,6 +200,8 @@
         send(own.at[0], meta.at[mine, k], sems(1), at_k(1))
 
     for d in range(1, group):
+        send(halves.at[seat], halves.at[seat], sems(8), at_seat(d))
+    for d in range(1, group):
         send(tall.at[seat], tall.at[seat], sems(3), at_seat(d))
     send(logs.at[:, k], logs.at[:, k], sems(4), at_k(1))
 
@@ -211,15 +225,8 @@
             send(piece, piece, (first_send.at[5], piece_sem.at[1, j]), at_x(d))
         return carry
 
-    lax.fori_loop(0, held, forward, 0)
-
-    def targets(tb):
-        at = tb % OWN * TILE
-        return tall[tb // OWN, at : at + TILE, :]
-
-    settle(tall.at[0 : group - 1], first_recv.at[3])
-    tgt_half = jnp.concatenate([half_norms(targets(tb)) for tb in range(blocks)], axis=0)
-    src_half = half_norms(src[...])
+    near = max(held - 3, 0)
+    lax.fori_loop(0, near, forward, 0)
 
     @pl.when(shift == 0)
     def _():
@@ -241,24 +248,37 @@
     )
 
     def stand(rows):
-        turned = jnp.transpose(rows)
-        for b in range(rows.shape[0]):
-            columns[b * TILE : (b + 1) * TILE, :] = jnp.broadcast_to(
-                turned[:, b : b + 1], (TILE, TILE)
-            )
+        n = rows.shape[0]
+        high = rows.astype(jnp.bfloat16).astype(jnp.float32)
+        rest = rows - high
+        middle = rest.astype(jnp.bfloat16).astype(jnp.float32)
+        pieces = jnp.concatenate([high, middle, rest - middle], axis=0)
+        turned = jnp.transpose(pieces).astype(jnp.bfloat16)
+        picks = picks_src if n == held else picks_tgt
+        spread = jnp.dot(turned, picks[...], preferred_element_type=jnp.float32)
+        for b in range(n):
+            columns[b * TILE : (b + 1) * TILE, :] = spread[:, b * TILE : (b + 1) * TILE]
 
     def first_half(i, carry):
-        j = slot_at(i)
+        pair_of = [slot_at(2 * i), slot_at(2 * i + 1)]
         if nx > 1:
-            settle(full.at[pl.ds(j * nx, nx - 1)], piece_sem.at[1, j])
-        source = full[pl.ds(j * nx, nx)].reshape(TILE, TILE)
-        for tb in range(blocks):
-            at = slice(tb * TILE, (tb + 1) * TILE)
-            tile = cross(targets(tb), source) * SCALE + bias[tb, pl.ds(j, 1), :]
-            ts_score[j, at, :] = tile
-            top, total = fold(tile + columns[at, :])
-            s_top[j, tb * 8 : (tb + 1) * 8, :] = top
-            s_sum[j, tb * 8 : (tb + 1) * 8, :] = total
+            for j in pair_of:
+                settle(full.at[pl.ds(j * nx, nx - 1)], piece_sem.at[1, j])
+        source = jnp.concatenate(
+            [full[pl.ds(j * nx, nx)].reshape(TILE, TILE) for j in pair_of], axis=0
+        )
+        for g in range(group):
+            product = cross(tall[g], source) * SCALE
+            for n in range(2 * OWN):
+                u, v = n // 2, n % 2
+                tb, j = OWN * g + u, pair_of[v]
+                at = slice(tb * TILE, (tb + 1) * TILE)
+                tile = product[u * TILE : (u + 1) * TILE, v * TILE : (v + 1) * TILE]
+                tile = tile + bias[tb, pl.ds(j, 1), :]
+                ts_score[j, at, :] = tile
+                top, total = fold(tile + columns[at, :])
+                s_top[j, tb * 8 : (tb + 1) * 8, :] = top
+                s_sum[j, tb * 8 : (tb + 1) * 8, :] = total
         return carry
 
     def source_half(j, carry):
@@ -272,8 +292,12 @@
     def build(j, carry):
         source = full[pl.ds(j * nx, nx)].reshape(TILE, TILE)
         rows = pl.ds(pl.multiple_of(j * TILE, TILE), TILE)
-        for tb in range(blocks):
-            st_score[tb, rows, :] = cross(source, targets(tb)) * SCALE + bias[tb, pl.ds(j, 1), :]
+        for g in range(group):
+            product = cross(source, tall[g]) * SCALE
+            for u in range(OWN):
+                tb = OWN * g + u
+                tile = product[:, u * TILE : (u + 1) * TILE]
+                st_score[tb, rows, :] = tile + bias[tb, pl.ds(j, 1), :]
         return carry
 
     def target_half(tb, carry):
@@ -287,10 +311,17 @@
     def pair(it, stage):
         return iter_send.at[it, stage], iter_recv.at[it, stage]
 
+    settle(halves.at[0 : group - 1], first_recv.at[8])
+    tgt_half = jnp.concatenate([halves[i] for i in range(group)], axis=0)
     tgt_pot = -tgt_half
     for it in range(ITERS):
         stand(tgt_pot)
-        lax.fori_loop(0, held, source_half if it else first_half, 0)
+        if it == 0:
+            lax.fori_loop(near, held, forward, 0)
+            settle(tall.at[0 : group - 1], first_recv.at[3])
+            lax.fori_loop(0, held // 2, first_half, 0)
+        else:
+            lax.fori_loop(0, held, source_half, 0)
         xbuf[it, x] = close(s_top[...], s_sum[...])
         for d in far_first(nx):
             send(xbuf.at[it, x], xbuf.at[it, x], pair(it, 0), at_x(d))
@@ -342,6 +373,7 @@
         settle(own.at[0], first_send.at[1])
 
     settle(tall.at[0 : group - 1], first_send.at[3])
+    settle(halves.at[0 : group - 1], first_send.at[8])
     settle(logs.at[:, 0], first_send.at[4])
     if nx > 1:
         settle(full.at[0 : held * (nx - 1)], first_send.at[5])
@@ -385,6 +417,9 @@
             pltpu.VMEM((held, nk, 1, 2 * TILE), f32),
             pltpu.VMEM((nz - 1, nk, 1, 2 * TILE), f32),
             pltpu.VMEM((ny, nk, OWN, TILE), f32),
+            pltpu.VMEM((group, OWN, TILE), f32),
+            pltpu.VMEM((3 * held, held * TILE), bf16),
+            pltpu.VMEM((3 * blocks, blocks * TILE), bf16),
             pltpu.VMEM((blocks, held, TILE), f32),
             pltpu.VMEM((held, blocks * TILE, TILE), f32),
             pltpu.VMEM((blocks, held * TILE, TILE), f32),
@@ -402,8 +437,8 @@
             pltpu.VMEM((nz, ny, OWN, TILE), f32),
             dma((6,)),
             dma((2, held)),
-            dma((8,)),
-            dma((8,)),
+            dma((9,)),
+            dma((9,)),
             dma((ITERS, 3)),
             dma((ITERS, 3)),
         ],

time: 96.4 us -> 94.8 us (0.983)
  Pallas kernels: 92.3 us -> 90.7 us
    pallas_call x1, Pallas kernels: 92.3 us -> 90.7 us  [body(): pl.pallas_call(functools.partial(kernel, dims), out_shape=(jax.ShapeDtype...]
where the time goes in v3:
time: 94.8 us; the launch traced here: 94.6 us
  Pallas kernels  90.7 us (96%)
  local copies, waits for them, and re-layouts  2.57 us (3%)
  between operations  1.29 us (1%)
    pallas_call x1, Pallas kernels, body(): pl.pallas_call(functools.partial(kernel, dims), out_shape=(jax.ShapeDtype...  90.7 us
    unnamed x4, local copies, waits for them, and re-layouts  2.57 us

profile of v3, /device:TPU:1, one launch (start us, length us, event | category | flops | bytes accessed | tf_op | source)
XLA Modules:
  0.0 94.6 jit_solution(17329638315714927861)
XLA Ops:
  1.3 90.7 %shard_map.77 = (f32[1,128]{1,0:T(1,128)}, f32[128,128]{1,0:T(8,128)}) custom-call(bf16[128,128]{1,0:T(8,128)(2,1)} %src_hbm.1, bf16[256,128]{1,0:T(8,128)(2,1)} %tgt_hbm.1, f32[1,128]{1,0:T(1,128)} %smass_hbm.1, f32[128,128]{1,0:T(8,128)} %tmass_hbm.1, s32[1,1,2,16]{3,2,1,0:T(2,128)} %list_hbm.1, s32[1,1]{1,0:T(1,128)S(6)} %copy.10.count_hbm), custom_call_target="tpu_custom_call" | custom-call | tf_op jit(solution)/shard_map/pallas_call | solution.py:400
  92.0 0.0 copy-start
  92.0 0.6 copy-done
  92.6 0.5 copy.11
  93.1 1.5 %copy.12 = f32[128,128]{1,0:T(8,128)} copy(f32[128,128]{1,0:T(8,128)} %get-tuple-element.5) | data formatting | bytes 131072
Async XLA Ops:
  92.0 0.6 copy-start

commit v4 on v3

--- a/solution.py
+++ b/solution.py
@@ -14,18 +14,19 @@
 SCALE = math.log2(math.e) / EPSILON
 TILE = 128
 OWN = 2
+SHARE = 4
+
+SRC_PARTS = 1
+TGT_PARTS = 2
 MESH = pl.DeviceIdType.MESH
-
 
 def far_first(count):
     return sorted(range(1, count), key=lambda d: (-min(d, count - d), d))
-
 
 def cross(left, right):
     return lax.dot_general(
         left, right, (((1,), (1,)), ((), ())), preferred_element_type=jnp.float32
     )
-
 
 def half_norms(points):
     wide = points.astype(jnp.float32)
@@ -36,23 +37,19 @@
     total = cross(ones, high) + cross(ones, low)
     return total[0:1] * (0.5 * SCALE)
 
-
 def merge(parts):
     top = jnp.max(parts, axis=0)
     return top + jnp.log2(jnp.sum(jnp.exp2(parts - top[None]), axis=0))
-
 
 def fold(s):
     s = s.reshape(s.shape[0] // 8, 8, TILE)
     top = jnp.max(s, axis=0)
     return top, jnp.sum(jnp.exp2(s - top[None]), axis=0)
 
-
 def close(tops, sums):
     top = jnp.max(tops, axis=1)
     total = jnp.sum(jnp.exp2(tops - top[:, None, :]) * sums, axis=1)
     return top + jnp.log2(total)
-
 
 def kernel(
     dims,
@@ -110,6 +107,8 @@
     x, k = lax.div(col, nk), lax.rem(col, nk)
     seat = y * nk + k
     mine = lax.div(z, nk)
+    src_part, tgt_part = held // SRC_PARTS, blocks // TGT_PARTS
+    src_share, tgt_share = min(SHARE, src_part), min(SHARE, tgt_part)
     shift = lax.rem(k + nz - lax.rem(z, nk), nk)
 
     def at_z(d):
@@ -247,17 +246,15 @@
         [logs[i // nk, i % nk] for i in range(group)], axis=0
     )
 
-    def stand(rows):
-        n = rows.shape[0]
+    def stand(rows, at, picks):
         high = rows.astype(jnp.bfloat16).astype(jnp.float32)
         rest = rows - high
         middle = rest.astype(jnp.bfloat16).astype(jnp.float32)
         pieces = jnp.concatenate([high, middle, rest - middle], axis=0)
         turned = jnp.transpose(pieces).astype(jnp.bfloat16)
-        picks = picks_src if n == held else picks_tgt
         spread = jnp.dot(turned, picks[...], preferred_element_type=jnp.float32)
-        for b in range(n):
-            columns[b * TILE : (b + 1) * TILE, :] = spread[:, b * TILE : (b + 1) * TILE]
+        for b in range(rows.shape[0]):
+            columns[(at + b) * TILE : (at + b + 1) * TILE, :] = spread[:, b * TILE : (b + 1) * TILE]
 
     def first_half(i, carry):
         pair_of = [slot_at(2 * i), slot_at(2 * i + 1)]
@@ -281,13 +278,18 @@
                 s_sum[j, tb * 8 : (tb + 1) * 8, :] = total
         return carry
 
-    def source_half(j, carry):
-        for tb in range(blocks):
-            at = slice(tb * TILE, (tb + 1) * TILE)
-            top, total = fold(ts_score[j, at, :] + columns[at, :])
-            s_top[j, tb * 8 : (tb + 1) * 8, :] = top
-            s_sum[j, tb * 8 : (tb + 1) * 8, :] = total
-        return carry
+    def source_half(first, last):
+        def run(step, carry):
+            for tb in range(first, last):
+                at = slice(tb * TILE, (tb + 1) * TILE)
+                column = columns[at, :]
+                for j in [src_share * step + n for n in range(src_share)]:
+                    top, total = fold(ts_score[j, at, :] + column)
+                    s_top[j, tb * 8 : (tb + 1) * 8, :] = top
+                    s_sum[j, tb * 8 : (tb + 1) * 8, :] = total
+            return carry
+
+        return run
 
     def build(j, carry):
         source = full[pl.ds(j * nx, nx)].reshape(TILE, TILE)
@@ -300,58 +302,95 @@
                 st_score[tb, rows, :] = tile + bias[tb, pl.ds(j, 1), :]
         return carry
 
-    def target_half(tb, carry):
-        for j in range(held):
-            at = slice(j * TILE, (j + 1) * TILE)
-            top, total = fold(st_score[tb, at, :] + columns[at, :])
-            t_top[tb, j * 8 : (j + 1) * 8, :] = top
-            t_sum[tb, j * 8 : (j + 1) * 8, :] = total
-        return carry
-
-    def pair(it, stage):
-        return iter_send.at[it, stage], iter_recv.at[it, stage]
+    def target_half(first, last):
+        def run(step, carry):
+            for j in range(first, last):
+                at = slice(j * TILE, (j + 1) * TILE)
+                column = columns[at, :]
+                for tb in [tgt_share * step + n for n in range(tgt_share)]:
+                    top, total = fold(st_score[tb, at, :] + column)
+                    t_top[tb, j * 8 : (j + 1) * 8, :] = top
+                    t_sum[tb, j * 8 : (j + 1) * 8, :] = total
+            return carry
+
+        return run
+
+    def pair(it, stage, p):
+        return iter_send.at[it, stage, p], iter_recv.at[it, stage, p]
+
+    def src_rows(p):
+        return slice(p * src_part, (p + 1) * src_part)
+
+    def tgt_rows(p):
+        return slice(p * tgt_part, (p + 1) * tgt_part)
+
+    def part_range(p, part, share):
+        return p * part // share, (p + 1) * part // share
+
+    def send_source(it, p):
+        xbuf[it, p, x] = close(s_top[src_rows(p)], s_sum[src_rows(p)])
+        for d in far_first(nx):
+            send(xbuf.at[it, p, x], xbuf.at[it, p, x], pair(it, 0, p), at_x(d))
+
+    def tgt_pot(it, p):
+        settle(ybuf.at[it, p, 0 : group - 1], iter_recv.at[it, 2, p])
+        return tgt_log[tgt_rows(p)] - merge(ybuf[it, p])
 
     settle(halves.at[0 : group - 1], first_recv.at[8])
     tgt_half = jnp.concatenate([halves[i] for i in range(group)], axis=0)
-    tgt_pot = -tgt_half
     for it in range(ITERS):
-        stand(tgt_pot)
         if it == 0:
+            for p in range(TGT_PARTS):
+                stand(-tgt_half[tgt_rows(p)], p * tgt_part, picks_tgt)
             lax.fori_loop(near, held, forward, 0)
             settle(tall.at[0 : group - 1], first_recv.at[3])
             lax.fori_loop(0, held // 2, first_half, 0)
+            for p in range(SRC_PARTS):
+                send_source(it, p)
         else:
-            lax.fori_loop(0, held, source_half, 0)
-        xbuf[it, x] = close(s_top[...], s_sum[...])
-        for d in far_first(nx):
-            send(xbuf.at[it, x], xbuf.at[it, x], pair(it, 0), at_x(d))
-        if nx > 1:
-            settle(xbuf.at[it, 0 : nx - 1], iter_recv.at[it, 0])
-        zbuf[it, z] = merge(xbuf[it])
-        for d in far_first(nz):
-            send(zbuf.at[it, z], zbuf.at[it, z], pair(it, 1), at_z(d))
+            for p in range(TGT_PARTS):
+                stand(tgt_pot(it - 1, p), p * tgt_part, picks_tgt)
+                if p < TGT_PARTS - 1:
+                    run = source_half(p * tgt_part, (p + 1) * tgt_part)
+                    lax.fori_loop(0, held // src_share, run, 0)
+            for p in range(SRC_PARTS):
+                run = source_half(blocks - tgt_part, blocks)
+                lax.fori_loop(*part_range(p, src_part, src_share), run, 0)
+                send_source(it, p)
+        for p in range(SRC_PARTS):
+            if nx > 1:
+                settle(xbuf.at[it, p, 0 : nx - 1], iter_recv.at[it, 0, p])
+            zbuf[it, p, z] = merge(xbuf[it, p])
+            for d in far_first(nz):
+                send(zbuf.at[it, p, z], zbuf.at[it, p, z], pair(it, 1, p), at_z(d))
         if it == 0:
             lax.fori_loop(0, held, build, 0)
-        settle(zbuf.at[it, 0 : nz - 1], iter_recv.at[it, 1])
-        src_pot = src_log - merge(zbuf[it])
-        stand(src_pot)
+        for p in range(SRC_PARTS):
+            settle(zbuf.at[it, p, 0 : nz - 1], iter_recv.at[it, 1, p])
+            src_pot = src_log[src_rows(p)] - merge(zbuf[it, p])
+            stand(src_pot, p * src_part, picks_src)
+            if it == ITERS - 1:
+                for n in range(src_part):
+                    qrow[p * src_part + n] = src_pot[n : n + 1, :]
+            if p < SRC_PARTS - 1:
+                run = target_half(p * src_part, (p + 1) * src_part)
+                lax.fori_loop(0, blocks // tgt_share, run, 0)
         if it == ITERS - 1:
-            for j in range(held):
-                qrow[j] = src_pot[j : j + 1, :]
 
             @pl.when(shift == 0)
             def _():
                 sib[0] = qrow[mine]
                 send(sib.at[0], sib.at[1], sems(6), at_k(1))
 
-        lax.fori_loop(0, blocks, target_half, 0)
-        ybuf[it, seat] = close(t_top[...], t_sum[...])
-        for d in range(1, group):
-            send(ybuf.at[it, seat], ybuf.at[it, seat], pair(it, 2), at_seat(d))
-        settle(ybuf.at[it, 0 : group - 1], iter_recv.at[it, 2])
-        tgt_pot = tgt_log - merge(ybuf[it])
-
-    result = (tgt_pot + tgt_half) * (1.0 / SCALE)
+        for p in range(TGT_PARTS):
+            run = target_half(held - src_part, held)
+            lax.fori_loop(*part_range(p, tgt_part, tgt_share), run, 0)
+            ybuf[it, p, seat] = close(t_top[tgt_rows(p)], t_sum[tgt_rows(p)])
+            for d in range(1, group):
+                send(ybuf.at[it, p, seat], ybuf.at[it, p, seat], pair(it, 2, p), at_seat(d))
+
+    last = jnp.concatenate([tgt_pot(ITERS - 1, p) for p in range(TGT_PARTS)], axis=0)
+    result = (last + tgt_half) * (1.0 / SCALE)
     for i in range(group):
         pots[i] = result[OWN * i : OWN * (i + 1), :]
     for yy in range(ny):
@@ -378,17 +417,18 @@
     if nx > 1:
         settle(full.at[0 : held * (nx - 1)], first_send.at[5])
     for it in range(ITERS):
-        if nx > 1:
-            settle(xbuf.at[it, 0 : nx - 1], iter_send.at[it, 0])
-        settle(zbuf.at[it, 0 : nz - 1], iter_send.at[it, 1])
-        settle(ybuf.at[it, 0 : group - 1], iter_send.at[it, 2])
+        for p in range(SRC_PARTS):
+            if nx > 1:
+                settle(xbuf.at[it, p, 0 : nx - 1], iter_send.at[it, 0, p])
+            settle(zbuf.at[it, p, 0 : nz - 1], iter_send.at[it, 1, p])
+        for p in range(TGT_PARTS):
+            settle(ybuf.at[it, p, 0 : group - 1], iter_send.at[it, 2, p])
     settle(obuf.at[0 : nz - 1], first_recv.at[7])
     settle(obuf.at[0 : nz - 1], first_send.at[7])
     for zz in range(nz):
         for yy in range(ny):
             at = OWN * (yy * nz + zz)
             otgt_ref[at : at + OWN, :] = obuf[zz, yy]
-
 
 def body(dims, *args):
     ny, nz, nx, nk = dims
@@ -418,8 +458,8 @@
             pltpu.VMEM((nz - 1, nk, 1, 2 * TILE), f32),
             pltpu.VMEM((ny, nk, OWN, TILE), f32),
             pltpu.VMEM((group, OWN, TILE), f32),
-            pltpu.VMEM((3 * held, held * TILE), bf16),
-            pltpu.VMEM((3 * blocks, blocks * TILE), bf16),
+            pltpu.VMEM((3 * held // SRC_PARTS, held // SRC_PARTS * TILE), bf16),
+            pltpu.VMEM((3 * blocks // TGT_PARTS, blocks // TGT_PARTS * TILE), bf16),
             pltpu.VMEM((blocks, held, TILE), f32),
             pltpu.VMEM((held, blocks * TILE, TILE), f32),
             pltpu.VMEM((blocks, held * TILE, TILE), f32),
@@ -428,9 +468,9 @@
             pltpu.VMEM((held, blocks * 8, TILE), f32),
             pltpu.VMEM((blocks, held * 8, TILE), f32),
             pltpu.VMEM((blocks, held * 8, TILE), f32),
-            pltpu.VMEM((ITERS, nx, held, TILE), f32),
-            pltpu.VMEM((ITERS, nz, held, TILE), f32),
-            pltpu.VMEM((ITERS, group, blocks, TILE), f32),
+            pltpu.VMEM((ITERS, SRC_PARTS, nx, held // SRC_PARTS, TILE), f32),
+            pltpu.VMEM((ITERS, SRC_PARTS, nz, held // SRC_PARTS, TILE), f32),
+            pltpu.VMEM((ITERS, TGT_PARTS, group, blocks // TGT_PARTS, TILE), f32),
             pltpu.VMEM((held, 1, TILE), f32),
             pltpu.VMEM((2, 1, TILE), f32),
             pltpu.VMEM((group, OWN, TILE), f32),
@@ -439,14 +479,13 @@
             dma((2, held)),
             dma((9,)),
             dma((9,)),
-            dma((ITERS, 3)),
-            dma((ITERS, 3)),
+            dma((ITERS, 3, max(SRC_PARTS, TGT_PARTS))),
+            dma((ITERS, 3, max(SRC_PARTS, TGT_PARTS))),
         ],
         compiler_params=pltpu.CompilerParams(
             collective_id=0, has_side_effects=True, vmem_limit_bytes=56 * 2**20
         ),
     )(*args)
-
 
 def solution(mesh, dims=(4, 16, 4, 2)):
     in_specs = (

time: 94.8 us -> 92.7 us (0.978)
  Pallas kernels: 90.7 us -> 88.6 us
    pallas_call x1, Pallas kernels: 90.7 us -> 88.6 us  [body(): pl.pallas_call(functools.partial(kernel, dims), out_shape=(jax.ShapeDtype...]
where the time goes in v4:
time: 92.7 us; the launch traced here: 92.5 us
  Pallas kernels  88.6 us (96%)
  local copies, waits for them, and re-layouts  2.57 us (3%)
  between operations  1.29 us (1%)
    pallas_call x1, Pallas kernels, body(): pl.pallas_call(functools.partial(kernel, dims), out_shape=(jax.ShapeDtype...  88.6 us
    unnamed x4, local copies, waits for them, and re-layouts  2.57 us

profile of v4, /device:TPU:1, one launch (start us, length us, event | category | flops | bytes accessed | tf_op | source)
XLA Modules:
  0.0 92.5 jit_solution(377737672583531741)
XLA Ops:
  1.3 88.6 %shard_map.77 = (f32[1,128]{1,0:T(1,128)}, f32[128,128]{1,0:T(8,128)}) custom-call(bf16[128,128]{1,0:T(8,128)(2,1)} %src_hbm.1, bf16[256,128]{1,0:T(8,128)(2,1)} %tgt_hbm.1, f32[1,128]{1,0:T(1,128)} %smass_hbm.1, f32[128,128]{1,0:T(8,128)} %tmass_hbm.1, s32[1,1,2,16]{3,2,1,0:T(2,128)} %list_hbm.1, s32[1,1]{1,0:T(1,128)S(6)} %copy.10.count_hbm), custom_call_target="tpu_custom_call" | custom-call | tf_op jit(solution)/shard_map/pallas_call | solution.py:440
  89.9 0.0 copy-start
  89.9 0.6 copy-done
  90.5 0.5 copy.11
  91.0 1.5 %copy.12 = f32[128,128]{1,0:T(8,128)} copy(f32[128,128]{1,0:T(8,128)} %get-tuple-element.5) | data formatting | bytes 131072
Async XLA Ops:
  89.9 0.6 copy-start

commit v5 on v4

--- a/solution.py
+++ b/solution.py
@@ -108,6 +108,7 @@
     seat = y * nk + k
     mine = lax.div(z, nk)
     src_part, tgt_part = held // SRC_PARTS, blocks // TGT_PARTS
+    far_seats = sorted(range(1, group), key=lambda d: abs(d - group / 2))
     src_share, tgt_share = min(SHARE, src_part), min(SHARE, tgt_part)
     shift = lax.rem(k + nz - lax.rem(z, nk), nk)
 
@@ -198,9 +199,9 @@
     def _():
         send(own.at[0], meta.at[mine, k], sems(1), at_k(1))
 
-    for d in range(1, group):
+    for d in far_seats:
         send(halves.at[seat], halves.at[seat], sems(8), at_seat(d))
-    for d in range(1, group):
+    for d in far_seats:
         send(tall.at[seat], tall.at[seat], sems(3), at_seat(d))
     send(logs.at[:, k], logs.at[:, k], sems(4), at_k(1))
 
@@ -386,7 +387,7 @@
             run = target_half(held - src_part, held)
             lax.fori_loop(*part_range(p, tgt_part, tgt_share), run, 0)
             ybuf[it, p, seat] = close(t_top[tgt_rows(p)], t_sum[tgt_rows(p)])
-            for d in range(1, group):
+            for d in far_seats:
                 send(ybuf.at[it, p, seat], ybuf.at[it, p, seat], pair(it, 2, p), at_seat(d))
 
     last = jnp.concatenate([tgt_pot(ITERS - 1, p) for p in range(TGT_PARTS)], axis=0)
@@ -483,7 +484,7 @@
             dma((ITERS, 3, max(SRC_PARTS, TGT_PARTS))),
         ],
         compiler_params=pltpu.CompilerParams(
-            collective_id=0, has_side_effects=True, vmem_limit_bytes=56 * 2**20
+            collective_id=0, has_side_effects=True, vmem_limit_bytes=55104 * 1024
         ),
     )(*args)
 

time: 92.7 us -> 91.2 us (0.984)
    unnamed x4 -> x8, local copies, waits for them, and re-layouts: 2.57 us -> 1.9 us
where the time goes in v5:
time: 91.2 us; the launch traced here: 90.9 us
  Pallas kernels  87.7 us (96%)
  local copies, waits for them, and re-layouts  1.9 us (2%)
  between operations  1.34 us (1%)
    pallas_call x1, Pallas kernels, body(): pl.pallas_call(functools.partial(kernel, dims), out_shape=(jax.ShapeDtype...  87.7 us
    unnamed x8, local copies, waits for them, and re-layouts  1.9 us

profile of v5, /device:TPU:1, one launch (start us, length us, event | category | flops | bytes accessed | tf_op | source)
XLA Modules:
  0.0 90.9 jit_solution(4450503381968426487)
XLA Ops:
  0.6 0.0 copy-start.1
  0.6 0.0 copy-start.2
  1.3 0.0 copy-done.1
  1.3 0.0 copy-done.2
  1.3 0.0 copy-start
  1.3 0.7 copy-done
  2.1 87.7 %shard_map.77 = (f32[1,128]{1,0:T(1,128)S(1)}, f32[128,128]{1,0:T(8,128)S(1)}) custom-call(bf16[128,128]{1,0:T(8,128)(2,1)S(1)} %copy-done, bf16[256,128]{1,0:T(8,128)(2,1)} %tgt_hbm.1, f32[1,128]{1,0:T(1,128)S(1)} %copy-done.2, f32[128,128]{1,0:T(8,128)} %tmass_hbm.1, s32[1,1,2,16]{3,2,1,0:T(2,128)S(1)} %copy-done.1, s32[1,1]{1,0:T(1,128)S(6)} %copy.10.count_hbm), custom_call_target="tpu_custom_call" | custom-call | tf_op jit(solution)/shard_map/pallas_call | solution.py:441
  89.8 0.5 copy.11
  90.3 0.6 copy.12
Async XLA Ops:
  0.6 0.7 copy-start.1
  0.6 0.7 copy-start.2
  1.3 0.8 copy-start

commit v6 on v5

--- a/solution.py
+++ b/solution.py
@@ -225,7 +225,7 @@
             send(piece, piece, (first_send.at[5], piece_sem.at[1, j]), at_x(d))
         return carry
 
-    near = max(held - 3, 0)
+    near = max(held - 2, 0)
     lax.fori_loop(0, near, forward, 0)
 
     @pl.when(shift == 0)

time: 91.2 us -> 90.8 us (level)
  no operation moved by 1% of the time
where the time goes in v6:
time: 90.8 us; the launch traced here: 90.6 us
  Pallas kernels  87.3 us (96%)
  local copies, waits for them, and re-layouts  1.9 us (2%)
  between operations  1.34 us (1%)
    pallas_call x1, Pallas kernels, body(): pl.pallas_call(functools.partial(kernel, dims), out_shape=(jax.ShapeDtype...  87.3 us
    unnamed x8, local copies, waits for them, and re-layouts  1.9 us

profile of v6, /device:TPU:1, one launch (start us, length us, event | category | flops | bytes accessed | tf_op | source)
XLA Modules:
  0.0 90.6 jit_solution(7324841964515151154)
XLA Ops:
  0.6 0.0 copy-start.1
  0.6 0.0 copy-start.2
  1.3 0.0 copy-done.1
  1.3 0.0 copy-done.2
  1.3 0.0 copy-start
  1.3 0.7 copy-done
  2.1 87.3 %shard_map.77 = (f32[1,128]{1,0:T(1,128)S(1)}, f32[128,128]{1,0:T(8,128)S(1)}) custom-call(bf16[128,128]{1,0:T(8,128)(2,1)S(1)} %copy-done, bf16[256,128]{1,0:T(8,128)(2,1)} %tgt_hbm.1, f32[1,128]{1,0:T(1,128)S(1)} %copy-done.2, f32[128,128]{1,0:T(8,128)} %tmass_hbm.1, s32[1,1,2,16]{3,2,1,0:T(2,128)S(1)} %copy-done.1, s32[1,1]{1,0:T(1,128)S(6)} %copy.10.count_hbm), custom_call_target="tpu_custom_call" | custom-call | tf_op jit(solution)/shard_map/pallas_call | solution.py:441
  89.4 0.5 copy.11
  90.0 0.6 copy.12
Async XLA Ops:
  0.6 0.7 copy-start.1
  0.6 0.7 copy-start.2
  1.3 0.8 copy-start
